TPU v7x, 32 devices: a whole 2x2x4 slice. The times are simulated.
32 devices in a mesh: group: 2 (over x), block: 16 (over z, y, core).
Axes of the slice: x: 2, y: 2, z: 4, core: 2. Of those that a mesh axis runs over, the one named last changes fastest.
Arguments:
- populations: float32 [19, 384, 8, 128], P(None, ('group', 'block')), parts along dimension 1, as said below
- design: float32 [384, 8, 128], P(('group', 'block')), parts along dimension 0, may hold values from 0.05 to 1
- fluid_mask: int32 [384, 8, 128], P(('group', 'block')), parts along dimension 0, may hold values 0 or 1
- owner_after: int32 [96], P('group'), parts along dimension 0, may hold values from 0 to 15, as said below
Outputs:
- populations_after: float32 [19, 640, 8, 128], P(None, ('group', 'block')), parts along dimension 1
- sensitivity: float32 [640, 8, 128], P(('group', 'block')), parts along dimension 0
There are 2 independent parts, one for each index of `group`. A program takes and returns all parts, laid end to end along the dimension named above; each array names one. Nothing has to cross between parts.
Inputs may be any that keep to these rules, and one draw needn't show every extreme that they name: `populations`: every population lies between 0.4 and 2.5 times its lattice weight. `owner_after`: the list never falls along the duct; every block goes to its home device (block index // 3) or a neighbour of it; every device owns from 1 to 5 blocks, and some device owns exactly 5; block 0 stays on device 0.
All inputs are finite; a program needn't handle non-finite values. No bound on the sum of `fluid_mask` on one device may be relied on, other than what follows from the above.
Results may differ from a plain program's by a relative error of at most 0.000021.
Values sent between devices are 32-bit elements; how exact they have to be, the bound alone decides.
No kernel may reach another device: no remote copies, remote signals or barrier semaphores. Data moves between devices by JAX's collectives and lax.ppermute only.
A program may use at most 64 MiB of HBM per device.

v0:
```python
from functools import partial

import jax
import jax.numpy as jnp
from jax import lax
from jax.sharding import PartitionSpec as P

BX = 4
STEPS = 3


velocity_set = (
    (0, 0, 0),
    (1, 0, 0),
    (-1, 0, 0),
    (0, 1, 0),
    (0, -1, 0),
    (0, 0, 1),
    (0, 0, -1),
    (1, 1, 0),
    (-1, -1, 0),
    (1, -1, 0),
    (-1, 1, 0),
    (1, 0, 1),
    (-1, 0, -1),
    (1, 0, -1),
    (-1, 0, 1),
    (0, 1, 1),
    (0, -1, -1),
    (0, 1, -1),
    (0, -1, 1),
)
weight_set = (1.0 / 3.0,) + (1.0 / 18.0,) * 6 + (1.0 / 36.0,) * 12
omega_rate = 1.2
alpha_top = 0.6
ramp_factor = 4.0
force_x = 0.02


def from_behind(block, axis, distance):
    devices = range(lax.axis_size(axis))
    route = [((i - distance) % len(devices), i) for i in devices]
    return lax.ppermute(block, axis, route)


def padded_2(cells, sides, width):
    for axis, dim in sides:
        count = lax.axis_size(axis)
        head = lax.slice_in_dim(cells, 0, width, axis=dim)
        tail = lax.slice_in_dim(cells, cells.shape[dim] - width, cells.shape[dim], axis=dim)
        cells = jnp.concatenate(
            [
                lax.ppermute(tail, axis, [(i, (i + 1) % count) for i in range(count)]),
                cells,
                lax.ppermute(head, axis, [((i + 1) % count, i) for i in range(count)]),
            ],
            axis=dim,
        )
    return cells


def opposite(member):
    if member == 0:
        return 0
    if member % 2 == 1:
        return member + 1
    return member - 1


def porosity(design):
    return alpha_top * (1.0 - design) / (1.0 + ramp_factor * design)


def moments(state):
    density = state[0]
    momentum = [jnp.zeros_like(density), jnp.zeros_like(density), jnp.zeros_like(density)]
    for member in range(1, 19):
        density = density + state[member]
        for coord in range(3):
            step = velocity_set[member][coord]
            if step == 1:
                momentum[coord] = momentum[coord] + state[member]
            elif step == -1:
                momentum[coord] = momentum[coord] - state[member]
    return (density, momentum)


def collide(state, design, fluid):
    density, momentum = moments(state)
    damping = 1.0 + porosity(design)
    speed_x = (momentum[0] / density + force_x) / damping
    speed_y = momentum[1] / density / damping
    speed_z = momentum[2] / density / damping
    square = speed_x * speed_x + speed_y * speed_y + speed_z * speed_z
    result = []
    for member in range(19):
        step_x, step_y, step_z = velocity_set[member]
        along = step_x * speed_x + step_y * speed_y + step_z * speed_z
        balance = (
            weight_set[member] * density * (1.0 + 3.0 * along + 4.5 * along * along - 1.5 * square)
        )
        result.append(state[member] - omega_rate * fluid * (state[member] - balance))
    return jnp.stack(result)


def drag_terms(state, design, fluid):
    density, momentum = moments(state)
    speed_x = momentum[0] / density
    speed_y = momentum[1] / density
    speed_z = momentum[2] / density
    return (
        fluid
        * (1.0 + porosity(design))
        * (speed_x * speed_x + speed_y * speed_y + speed_z * speed_z)
    )


def shifted_yz(field, step_y, step_z):
    padded = jnp.pad(field, ((0, 0), (1, 1), (1, 1)))
    width_y = field.shape[1]
    width_z = field.shape[2]
    return padded[:, 1 - step_y : 1 - step_y + width_y, 1 - step_z : 1 - step_z + width_z]


def from_below(field, edge):
    return jnp.concatenate([edge[None], field[:-1]], axis=0)


def from_above(field, edge, last_plane):
    moved = jnp.concatenate([field[1:], jnp.zeros_like(field[:1])], axis=0)
    return lax.dynamic_update_slice_in_dim(moved, edge[None], last_plane, 0)


def faces(send_right, send_left):
    from_left = from_behind(send_right, "block", 1)
    from_right = from_behind(send_left, "block", -1)
    return (from_left, from_right)


def swap_faces(field, last_plane, right_members, left_members):
    plane_last = lax.dynamic_index_in_dim(field, last_plane, 1, keepdims=False)
    send_right = jnp.stack([plane_last[member] for member in right_members])
    send_left = jnp.stack([field[member, 0] for member in left_members])
    from_left, from_right = faces(send_right, send_left)
    left_planes = {member: from_left[place] for place, member in enumerate(right_members)}
    right_planes = {member: from_right[place] for place, member in enumerate(left_members)}
    return (left_planes, right_planes)


def drag_seed(partial_drag, cell_total):
    total = lax.psum(partial_drag, "block")
    return cell_total / total


def body(populations, design, fluid_mask, owner_after):
    count_dev = lax.axis_size("block")
    rank = lax.axis_index("block")
    home_planes = design.shape[0]
    width_y = design.shape[1]
    width_z = design.shape[2]
    home_blocks = home_planes // BX
    planes = (home_blocks + 2) * BX
    all_members = tuple(range(19))
    ahead, behind = (all_members, all_members)
    start_block = jnp.sum((owner_after < rank).astype(jnp.int32))
    own_blocks = jnp.sum((owner_after == rank).astype(jnp.int32))
    last_plane = own_blocks * BX - 1
    cell_total = jnp.float32(count_dev * home_planes * width_y * width_z)
    marked = jnp.where(fluid_mask > 0, design, -1.0)
    stacked = jnp.concatenate([populations, marked[None]], axis=0)
    weight_column = jnp.array(weight_set, jnp.float32)[:, None, None, None]
    plane_ids = lax.broadcasted_iota(jnp.int32, (planes, width_y, width_z), 0)
    live = (plane_ids <= last_plane).astype(jnp.float32)
    anchor = (start_block - rank * home_blocks + 1) * BX
    widened = padded_2(stacked, (("block", 1),), BX + 1)
    widened = jnp.concatenate(
        [widened, jnp.zeros((20, 2 * BX, width_y, width_z), jnp.float32)], axis=1
    )
    window = lax.dynamic_slice_in_dim(widened, anchor, planes + 2, 1)
    inner = window[:, 1 : planes + 1]
    fluid = jnp.where(inner[19] >= 0.0, live, 0.0)
    design_local = jnp.maximum(inner[19], 0.0)
    state = jnp.where(live[None] > 0.0, inner[:19], weight_column)
    fluid_left = (window[19, 0] >= 0.0).astype(jnp.float32)
    fluid_right = (
        lax.dynamic_index_in_dim(window[19], last_plane + 2, 0, keepdims=False) >= 0.0
    ).astype(jnp.float32)
    sources = []
    for member in range(19):
        step_x, step_y, step_z = velocity_set[member]
        if step_x == 1:
            moved = from_below(fluid, fluid_left)
        elif step_x == -1:
            moved = from_above(fluid, fluid_right, last_plane)
        else:
            moved = fluid
        sources.append(shifted_yz(moved, step_y, step_z))

    def stream_adjoint(adjoint):
        carried = jnp.stack([fluid * sources[member] * adjoint[member] for member in range(19)])
        left_planes, right_planes = swap_faces(carried, last_plane, behind, ahead)
        result = []
        for member in range(19):
            step_x, step_y, step_z = velocity_set[member]
            if step_x == 1:
                moved = from_above(carried[member], right_planes[member], last_plane)
            elif step_x == -1:
                moved = from_below(carried[member], left_planes[member])
            else:
                moved = carried[member]
            moved = shifted_yz(moved, -step_y, -step_z)
            mirror = opposite(member)
            result.append(
                moved
                + fluid * (1.0 - sources[mirror]) * adjoint[mirror]
                + (1.0 - fluid) * adjoint[member]
            )
        return jnp.stack(result)

    def local_drag(state_here, design_here):
        return jnp.sum(drag_terms(state_here, design_here, fluid))

    history = []
    current = state
    for step in range(STEPS):
        history.append(current)
        collided = collide(current, design_local, fluid)
        stream_left_planes, stream_right_planes = swap_faces(collided, last_plane, ahead, behind)
        stream_result = []
        for stream_member in range(19):
            stream_step_x, stream_step_y, stream_step_z = velocity_set[stream_member]
            if stream_step_x == 1:
                stream_moved = from_below(
                    collided[stream_member], stream_left_planes[stream_member]
                )
            elif stream_step_x == -1:
                stream_moved = from_above(
                    collided[stream_member], stream_right_planes[stream_member], last_plane
                )
            else:
                stream_moved = collided[stream_member]
            stream_moved = shifted_yz(stream_moved, stream_step_y, stream_step_z)
            source = sources[stream_member]
            stream_result.append(
                fluid * (source * stream_moved + (1.0 - source) * collided[opposite(stream_member)])
                + (1.0 - fluid) * collided[stream_member]
            )
        current = jnp.stack(stream_result)
    partial_drag = local_drag(current, design_local)
    seed = drag_seed(partial_drag, cell_total)
    value, pull_back = jax.vjp(local_drag, current, design_local)
    adjoint, gradient = pull_back(seed)
    collide_here = partial(collide, fluid=fluid)
    for step in reversed(range(STEPS)):
        through = stream_adjoint(adjoint)
        value, pull_back = jax.vjp(collide_here, history[step], design_local)
        adjoint, extra = pull_back(through)
        gradient = gradient + extra
    final = jnp.where(live[None] > 0.0, current, 0.0)
    return (final, gradient * live)


def solution(mesh):
    placed = (
        P(None, ("group", "block"), None, None),
        P(("group", "block"), None, None),
        P(("group", "block"), None, None),
        P("group"),
    )
    return jax.shard_map(
        body,
        mesh=mesh,
        in_specs=placed,
        out_specs=(P(None, ("group", "block"), None, None), P(("group", "block"), None, None)),
        check_vma=False,
    )
```

profile of v0, /device:TPU:0, one launch (start us, length us, event | category | flops | bytes accessed | tf_op | source)
XLA Modules:
  0.0 147.7 jit_solution(3239245894862259645)
XLA Ops:
  0.6 0.8 select_bitcast_fusion
  1.5 1.2 pad_maximum_fusion
  2.7 5.5 %collective-permute-start.1 = (f32[20,5,8,128]{3,2,1,0:T(8,128)S(1)}, f32[20,5,8,128]{3,2,1,0:T(8,128)S(1)}, u32[]{:S(2)}, u32[]{:S(2)}) collective-permute-start(f32[20,5,8,128]{3,2,1,0:T(8,128)S(1)} %get-tuple-element.562), channel_id=1, source_target_pairs={{1,0},{2,1},{3,2},{4,3},{5,4},{6,5},{7,6},{8,7},{9,8},{10,9},{11,1... | collective-permute-start | bytes 1228808 | tf_op jit(solution)/shard_map/ppermute | solution.py:55
  10.7 2.9 %collective-permute-done.1 = f32[20,5,8,128]{3,2,1,0:T(8,128)S(1)} collective-permute-done((f32[20,5,8,128]{3,2,1,0:T(8,128)S(1)}, f32[20,5,8,128]{3,2,1,0:T(8,128)S(1)}, u32[]{:S(2)}, u32[]{:S(2)}) %collective-permute-start.1) | collective-permute-done | bytes 409632 | tf_op jit(solution)/shard_map/ppermute | solution.py:55
  13.6 4.6 %collective-permute-done = f32[20,5,8,128]{3,2,1,0:T(8,128)S(1)} collective-permute-done((f32[20,5,8,128]{3,2,1,0:T(8,128)S(1)}, f32[20,5,8,128]{3,2,1,0:T(8,128)S(1)}, u32[]{:S(2)}, u32[]{:S(2)}) %collective-permute-start) | collective-permute-done | bytes 409632 | tf_op jit(solution)/shard_map/ppermute | solution.py:53
  18.2 1.6 %fusion.228 = f32[20,22,8,128]{3,2,1,0:T(8,128)S(1)} fusion(s32[]{:T(128)S(6)} %select_n.103, f32[20,5,8,128]{3,2,1,0:T(8,128)S(1)} %collective-permute-done, f32[19,12,8,128]{3,2,1,0:T(8,128)} %param.5, f32[1,12,8,128]{3,2,1,0:T(8,128)S(1)} %select_bitcast_fusion, f32[20,5,8,128]{3,2,1,0:T(8,128)S(1)} %collective-permute-done.1, ...), kind=kLoop, calls=%fused_computation.334 | loop fusion | flops 1802240 | bytes 3604572 | tf_op jit(solution)/shard_map/concatenate | solution.py:176
  20.0 1.1 fusion.979
  22.1 0.9 select_multiply_fusion.2
  25.5 4.4 %collective-permute-start.3 = (f32[19,8,128]{2,1,0:T(8,128)S(1)}, f32[19,8,128]{2,1,0:T(8,128)S(1)}, u32[]{:S(2)}, u32[]{:S(2)}) collective-permute-start(f32[19,8,128]{2,1,0:T(8,128)S(1)} %constant_dynamic-update-slice_fusion.38), channel_id=1, source_target_pairs={{1,0},{2,1},{3,2},{4,3},{5,4},{6,5},{7,6},{8,7},{9,8},{10,9},{11,1... | collective-permute-start | bytes 233480 | tf_op jit(solution)/shard_map/ppermute | solution.py:43
  30.0 1.9 %collective-permute-done.2 = f32[19,8,128]{2,1,0:T(8,128)S(1)} collective-permute-done((f32[19,8,128]{2,1,0:T(8,128)S(1)}, f32[19,8,128]{2,1,0:T(8,128)S(1)}, u32[]{:S(2)}, u32[]{:S(2)}) %collective-permute-start.2) | collective-permute-done | bytes 77856 | tf_op jit(solution)/shard_map/ppermute | solution.py:43
  32.0 1.5 %constant_dynamic-update-slice_fusion.75 = (f32[19,20,8,128]{3,2,1,0:T(8,128)S(1)}, f32[20,8,128]{2,1,0:T(8,128)S(1)}, f32[20,8,128]{2,1,0:T(8,128)S(1)}, f32[20...) fusion(f32[20,8,128]{2,1,0:T(8,128)S(1)} %get-tuple-element.434, ...), kind=kLoop, calls=%fused_computation.424 | loop fusion | flops 5324799 | bytes 5263440
  41.2 4.5 %collective-permute-start.5 = (f32[19,8,128]{2,1,0:T(8,128)S(1)}, f32[19,8,128]{2,1,0:T(8,128)S(1)}, u32[]{:S(2)}, u32[]{:S(2)}) collective-permute-start(f32[19,8,128]{2,1,0:T(8,128)S(1)} %constant_dynamic-update-slice_fusion.95), channel_id=1, source_target_pairs={{1,0},{2,1},{3,2},{4,3},{5,4},{6,5},{7,6},{8,7},{9,8},{10,9},{11,1... | collective-permute-start | bytes 233480 | tf_op jit(solution)/shard_map/ppermute | solution.py:43
  45.7 1.6 %collective-permute-done.4 = f32[19,8,128]{2,1,0:T(8,128)S(1)} collective-permute-done((f32[19,8,128]{2,1,0:T(8,128)S(1)}, f32[19,8,128]{2,1,0:T(8,128)S(1)}, u32[]{:S(2)}, u32[]{:S(2)}) %collective-permute-start.4) | collective-permute-done | bytes 77856 | tf_op jit(solution)/shard_map/ppermute | solution.py:43
  47.7 1.5 %constant_dynamic-update-slice_fusion.132 = (f32[19,20,8,128]{3,2,1,0:T(8,128)S(1)}, f32[20,8,128]{2,1,0:T(8,128)S(1)}, f32[20,8,128]{2,1,0:T(8,128)S(1)}, f32[2...) fusion(f32[20,8,128]{2,1,0:T(8,128)S(1)} %get-tuple-element.405, ...), kind=kLoop, calls=%fused_computation.481 | loop fusion | flops 5427199 | bytes 5263440
  56.9 4.6 %collective-permute-start.7 = (f32[19,8,128]{2,1,0:T(8,128)S(1)}, f32[19,8,128]{2,1,0:T(8,128)S(1)}, u32[]{:S(2)}, u32[]{:S(2)}) collective-permute-start(f32[19,8,128]{2,1,0:T(8,128)S(1)} %constant_dynamic-update-slice_fusion.152), channel_id=1, source_target_pairs={{1,0},{2,1},{3,2},{4,3},{5,4},{6,5},{7,6},{8,7},{9,8},{10,9},{11,1... | collective-permute-start | bytes 233480 | tf_op jit(solution)/shard_map/ppermute | solution.py:43
  61.5 1.6 %collective-permute-done.6 = f32[19,8,128]{2,1,0:T(8,128)S(1)} collective-permute-done((f32[19,8,128]{2,1,0:T(8,128)S(1)}, f32[19,8,128]{2,1,0:T(8,128)S(1)}, u32[]{:S(2)}, u32[]{:S(2)}) %collective-permute-start.6) | collective-permute-done | bytes 77856 | tf_op jit(solution)/shard_map/ppermute | solution.py:43
  63.5 2.6 %multiply_reduce_fusion = (f32[]{:T(128)}, f32[20,8,128]{2,1,0:T(8,128)}, f32[20,8,128]{2,1,0:T(8,128)}, f32[20,8,128]{2,1,0:T(8,128)}, f32[20,8,128]{2,1,0:T(8,...) fusion(f32[20]{0:T(128)S(1)} %get-tuple-element.649, ...), kind=kLoop, calls=%fused_computation.2112 | loop fusion | flops 5058559 | bytes 4690004 | tf_op jit(solution)/shard_map/reduce_sum | solution.py:221
  66.1 35.0 %psum.7 = f32[]{:T(128)} all-reduce(f32[]{:T(128)} %get-tuple-element.252), channel_id=1, replica_groups=mesh['group'=2,'block'=16] {'block'}, use_global_device_ids=true, to_apply=%region_3.4 | all-reduce | flops 1 | bytes 8 | tf_op jit(solution)/shard_map/psum | solution.py:151
  101.8 1.1 negate_bitcast_fusion.7
  106.6 4.5 %collective-permute-start.9 = (f32[19,8,128]{2,1,0:T(8,128)S(1)}, f32[19,8,128]{2,1,0:T(8,128)S(1)}, u32[]{:S(2)}, u32[]{:S(2)}) collective-permute-start(f32[19,8,128]{2,1,0:T(8,128)S(1)} %constant_dynamic-update-slice_fusion.228), channel_id=1, source_target_pairs={{1,0},{2,1},{3,2},{4,3},{5,4},{6,5},{7,6},{8,7},{9,8},{10,9},{11,1... | collective-permute-start | bytes 233480 | tf_op jit(solution)/shard_map/ppermute | solution.py:43
  111.1 1.1 collective-permute-done.8
  114.5 0.9 negate_bitcast_fusion.4
  117.3 0.8 pad_add_fusion.1
  121.5 4.6 %collective-permute-start.11 = (f32[19,8,128]{2,1,0:T(8,128)S(1)}, f32[19,8,128]{2,1,0:T(8,128)S(1)}, u32[]{:S(2)}, u32[]{:S(2)}) collective-permute-start(f32[19,8,128]{2,1,0:T(8,128)S(1)} %constant_dynamic-update-slice_fusion.285), channel_id=1, source_target_pairs={{1,0},{2,1},{3,2},{4,3},{5,4},{6,5},{7,6},{8,7},{9,8},{10,9},{11,1... | collective-permute-start | bytes 233480 | tf_op jit(solution)/shard_map/ppermute | solution.py:43
  126.0 1.1 collective-permute-done.10
  129.5 0.9 negate_bitcast_fusion.1
  131.5 0.8 fusion.1167
  132.3 0.8 pad_add_fusion
  136.4 1.4 broadcast_select_fusion
  138.2 4.6 %collective-permute-start.13 = (f32[19,8,128]{2,1,0:T(8,128)S(1)}, f32[19,8,128]{2,1,0:T(8,128)S(1)}, u32[]{:S(2)}, u32[]{:S(2)}) collective-permute-start(f32[19,8,128]{2,1,0:T(8,128)S(1)} %constant_dynamic-update-slice_fusion.342), channel_id=1, source_target_pairs={{1,0},{2,1},{3,2},{4,3},{5,4},{6,5},{7,6},{8,7},{9,8},{10,9},{11,1... | collective-permute-start | bytes 233480 | tf_op jit(solution)/shard_map/ppermute | solution.py:43
  142.8 2.0 %collective-permute-done.13 = f32[19,8,128]{2,1,0:T(8,128)S(1)} collective-permute-done((f32[19,8,128]{2,1,0:T(8,128)S(1)}, f32[19,8,128]{2,1,0:T(8,128)S(1)}, u32[]{:S(2)}, u32[]{:S(2)}) %collective-permute-start.13) | collective-permute-done | bytes 77856 | tf_op jit(solution)/shard_map/ppermute | solution.py:43
  144.9 2.8 %fusion.1124 = f32[20,8,128]{2,1,0:T(8,128)} fusion(f32[20,8,128]{2,1,0:T(8,128)S(1)} %copy-done.47, f32[20,8,128]{2,1,0:T(8,128)S(1)} %copy-done.13, f32[20,8,128]{2,1,0:T(8,128)S(1)} %copy-done.48, f32[20,8,128]{2,1,0:T(8,128)S(1)} %copy-done.19, f32[20,8,128]{2,1,0:T(8,128)S(1)} %copy-done.15, f32[20,8,128]{2,1,0:T(8,128)S(1)} %copy-done.49, ...), kind=kLoop, calls=%fused_computation.1960 | loop fusion | flops 12963840 | bytes 5345384 | tf_op jit(solution)/shard_map/mul | solution.py:260
  (656 shorter events, 35.9 us)
Async XLA Ops:
  0.6 7.5 %copy-start.71 = (s32[48]{0:T(128)S(1)}, s32[48]{0:T(128)}, u32[]{:S(2)}) copy-start(s32[48]{0:T(128)} %param.8) | copy-start | bytes 580
  2.7 11.0 %collective-permute-start.1 = (f32[20,5,8,128]{3,2,1,0:T(8,128)S(1)}, f32[20,5,8,128]{3,2,1,0:T(8,128)S(1)}, u32[]{:S(2)}, u32[]{:S(2)}) collective-permute-start(f32[20,5,8,128]{3,2,1,0:T(8,128)S(1)} %get-tuple-element.562), channel_id=1, source_target_pairs={{1,0},{2,1},{3,2},{4,3},{5,4},{6,5},{7,6},{8,7},{9,8},{10,9},{11,1... | collective-permute-start | bytes 1228808 | tf_op jit(solution)/shard_map/ppermute | solution.py:55
  8.2 10.1 %collective-permute-start = (f32[20,5,8,128]{3,2,1,0:T(8,128)S(1)}, f32[20,5,8,128]{3,2,1,0:T(8,128)S(1)}, u32[]{:S(2)}, u32[]{:S(2)}) collective-permute-start(f32[20,5,8,128]{3,2,1,0:T(8,128)S(1)} %get-tuple-element.563), channel_id=1, source_target_pairs={{0,1},{1,2},{2,3},{3,4},{4,5},{5,6},{6,7},{7,8},{8,9},{9,10},{10,1... | collective-permute-start | bytes 1228808 | tf_op jit(solution)/shard_map/ppermute | solution.py:53
  10.7 9.1 %copy-start.69 = (pred[20]{0:T(512)(128)(4,1)}, pred[20]{0:T(512)(128)(4,1)S(1)}, u32[]{:S(2)}) copy-start(pred[20]{0:T(512)(128)(4,1)S(1)} %get-tuple-element.648) | copy-start | bytes 64
  10.7 9.1 %copy-start.72 = (f32[19]{0:T(128)S(1)}, f32[19]{0:T(128)}, u32[]{:S(2)}) copy-start(f32[19]{0:T(128)} %constant.82.clone) | copy-start | bytes 232
  24.5 5.5 %slice-start = ((f32[20,22,8,128]{3,2,1,0:T(8,128)}), f32[1,22,8,128]{3,2,1,0:T(8,128)S(1)}, s32[]{:S(2)}) async-start(f32[20,22,8,128]{3,2,1,0:T(8,128)} %copy-done), calls=%async_computation | async-start | bytes 180224 | tf_op jit(solution)/shard_map/slice | solution.py:186
  24.5 7.5 %copy-start.1 = (f32[20,22,8,128]{3,2,1,0:T(8,128)S(1)}, f32[20,22,8,128]{3,2,1,0:T(8,128)}, u32[]{:S(2)}) copy-start(f32[20,22,8,128]{3,2,1,0:T(8,128)} %copy-done) | copy-start | bytes 5406724
  25.3 6.6 %collective-permute-start.2 = (f32[19,8,128]{2,1,0:T(8,128)S(1)}, f32[19,8,128]{2,1,0:T(8,128)S(1)}, u32[]{:S(2)}, u32[]{:S(2)}) collective-permute-start(f32[19,8,128]{2,1,0:T(8,128)S(1)} %constant_dynamic-update-slice_fusion.19), channel_id=1, source_target_pairs={{15,0},{0,1},{1,2},{2,3},{3,4},{4,5},{5,6},{6,7},{7,8},{8,9},{9,10... | collective-permute-start | bytes 233480 | tf_op jit(solution)/shard_map/ppermute | solution.py:43
  25.5 6.5 %collective-permute-start.3 = (f32[19,8,128]{2,1,0:T(8,128)S(1)}, f32[19,8,128]{2,1,0:T(8,128)S(1)}, u32[]{:S(2)}, u32[]{:S(2)}) collective-permute-start(f32[19,8,128]{2,1,0:T(8,128)S(1)} %constant_dynamic-update-slice_fusion.38), channel_id=1, source_target_pairs={{1,0},{2,1},{3,2},{4,3},{5,4},{6,5},{7,6},{8,7},{9,8},{10,9},{11,1... | collective-permute-start | bytes 233480 | tf_op jit(solution)/shard_map/ppermute | solution.py:43
  40.7 6.6 %collective-permute-start.4 = (f32[19,8,128]{2,1,0:T(8,128)S(1)}, f32[19,8,128]{2,1,0:T(8,128)S(1)}, u32[]{:S(2)}, u32[]{:S(2)}) collective-permute-start(f32[19,8,128]{2,1,0:T(8,128)S(1)} %constant_dynamic-update-slice_fusion.76), channel_id=1, source_target_pairs={{15,0},{0,1},{1,2},{2,3},{3,4},{4,5},{5,6},{6,7},{7,8},{8,9},{9,10... | collective-permute-start | bytes 233480 | tf_op jit(solution)/shard_map/ppermute | solution.py:43
  41.2 6.6 %collective-permute-start.5 = (f32[19,8,128]{2,1,0:T(8,128)S(1)}, f32[19,8,128]{2,1,0:T(8,128)S(1)}, u32[]{:S(2)}, u32[]{:S(2)}) collective-permute-start(f32[19,8,128]{2,1,0:T(8,128)S(1)} %constant_dynamic-update-slice_fusion.95), channel_id=1, source_target_pairs={{1,0},{2,1},{3,2},{4,3},{5,4},{6,5},{7,6},{8,7},{9,8},{10,9},{11,1... | collective-permute-start | bytes 233480 | tf_op jit(solution)/shard_map/ppermute | solution.py:43
  49.2 14.3 %copy-start.21 = (f32[20,8,128]{2,1,0:T(8,128)}, f32[20,8,128]{2,1,0:T(8,128)S(1)}, u32[]{:S(2)}) copy-start(f32[20,8,128]{2,1,0:T(8,128)S(1)} %get-tuple-element.326) | copy-start | bytes 245764
  49.5 5.8 %copy-start.2 = (f32[20,8,128]{2,1,0:T(8,128)}, f32[20,8,128]{2,1,0:T(8,128)S(1)}, u32[]{:S(2)}) copy-start(f32[20,8,128]{2,1,0:T(8,128)S(1)} %get-tuple-element.318) | copy-start | bytes 245764
  49.7 5.8 %copy-start.4 = (f32[20,8,128]{2,1,0:T(8,128)}, f32[20,8,128]{2,1,0:T(8,128)S(1)}, u32[]{:S(2)}) copy-start(f32[20,8,128]{2,1,0:T(8,128)S(1)} %get-tuple-element.315) | copy-start | bytes 245764
  56.4 6.6 %collective-permute-start.6 = (f32[19,8,128]{2,1,0:T(8,128)S(1)}, f32[19,8,128]{2,1,0:T(8,128)S(1)}, u32[]{:S(2)}, u32[]{:S(2)}) collective-permute-start(f32[19,8,128]{2,1,0:T(8,128)S(1)} %constant_dynamic-update-slice_fusion.133), channel_id=1, source_target_pairs={{15,0},{0,1},{1,2},{2,3},{3,4},{4,5},{5,6},{6,7},{7,8},{8,9},{9,10... | collective-permute-start | bytes 233480 | tf_op jit(solution)/shard_map/ppermute | solution.py:43
  56.9 6.6 %collective-permute-start.7 = (f32[19,8,128]{2,1,0:T(8,128)S(1)}, f32[19,8,128]{2,1,0:T(8,128)S(1)}, u32[]{:S(2)}, u32[]{:S(2)}) collective-permute-start(f32[19,8,128]{2,1,0:T(8,128)S(1)} %constant_dynamic-update-slice_fusion.152), channel_id=1, source_target_pairs={{1,0},{2,1},{3,2},{4,3},{5,4},{6,5},{7,6},{8,7},{9,8},{10,9},{11,1... | collective-permute-start | bytes 233480 | tf_op jit(solution)/shard_map/ppermute | solution.py:43
  105.6 6.6 %collective-permute-start.8 = (f32[19,8,128]{2,1,0:T(8,128)S(1)}, f32[19,8,128]{2,1,0:T(8,128)S(1)}, u32[]{:S(2)}, u32[]{:S(2)}) collective-permute-start(f32[19,8,128]{2,1,0:T(8,128)S(1)} %constant_dynamic-update-slice_fusion.209), channel_id=1, source_target_pairs={{15,0},{0,1},{1,2},{2,3},{3,4},{4,5},{5,6},{6,7},{7,8},{8,9},{9,10... | collective-permute-start | bytes 233480 | tf_op jit(solution)/shard_map/ppermute | solution.py:43
  106.4 6.0 %copy-start.20 = (f32[20,8,128]{2,1,0:T(8,128)S(1)}, f32[20,8,128]{2,1,0:T(8,128)}, u32[]{:S(2)}) copy-start(f32[20,8,128]{2,1,0:T(8,128)} %get-tuple-element.574) | copy-start | bytes 245764
  106.6 6.5 %collective-permute-start.9 = (f32[19,8,128]{2,1,0:T(8,128)S(1)}, f32[19,8,128]{2,1,0:T(8,128)S(1)}, u32[]{:S(2)}, u32[]{:S(2)}) collective-permute-start(f32[19,8,128]{2,1,0:T(8,128)S(1)} %constant_dynamic-update-slice_fusion.228), channel_id=1, source_target_pairs={{1,0},{2,1},{3,2},{4,3},{5,4},{6,5},{7,6},{8,7},{9,8},{10,9},{11,1... | collective-permute-start | bytes 233480 | tf_op jit(solution)/shard_map/ppermute | solution.py:43
  120.5 6.6 %collective-permute-start.10 = (f32[19,8,128]{2,1,0:T(8,128)S(1)}, f32[19,8,128]{2,1,0:T(8,128)S(1)}, u32[]{:S(2)}, u32[]{:S(2)}) collective-permute-start(f32[19,8,128]{2,1,0:T(8,128)S(1)} %constant_dynamic-update-slice_fusion.266), channel_id=1, source_target_pairs={{15,0},{0,1},{1,2},{2,3},{3,4},{4,5},{5,6},{6,7},{7,8},{8,9},{9,10... | collective-permute-start | bytes 233480 | tf_op jit(solution)/shard_map/ppermute | solution.py:43
  121.5 6.6 %collective-permute-start.11 = (f32[19,8,128]{2,1,0:T(8,128)S(1)}, f32[19,8,128]{2,1,0:T(8,128)S(1)}, u32[]{:S(2)}, u32[]{:S(2)}) collective-permute-start(f32[19,8,128]{2,1,0:T(8,128)S(1)} %constant_dynamic-update-slice_fusion.285), channel_id=1, source_target_pairs={{1,0},{2,1},{3,2},{4,3},{5,4},{6,5},{7,6},{8,7},{9,8},{10,9},{11,1... | collective-permute-start | bytes 233480 | tf_op jit(solution)/shard_map/ppermute | solution.py:43
  135.7 7.0 %collective-permute-start.12 = (f32[19,8,128]{2,1,0:T(8,128)S(1)}, f32[19,8,128]{2,1,0:T(8,128)S(1)}, u32[]{:S(2)}, u32[]{:S(2)}) collective-permute-start(f32[19,8,128]{2,1,0:T(8,128)S(1)} %constant_dynamic-update-slice_fusion.323), channel_id=1, source_target_pairs={{15,0},{0,1},{1,2},{2,3},{3,4},{4,5},{5,6},{6,7},{7,8},{8,9},{9,10... | collective-permute-start | bytes 233480 | tf_op jit(solution)/shard_map/ppermute | solution.py:43
  137.7 7.1 %copy-start.13 = (f32[20,8,128]{2,1,0:T(8,128)S(1)}, f32[20,8,128]{2,1,0:T(8,128)}, u32[]{:S(2)}) copy-start(f32[20,8,128]{2,1,0:T(8,128)} %copy-done.12) | copy-start | bytes 245764
  137.7 7.1 %copy-start.15 = (f32[20,8,128]{2,1,0:T(8,128)S(1)}, f32[20,8,128]{2,1,0:T(8,128)}, u32[]{:S(2)}) copy-start(f32[20,8,128]{2,1,0:T(8,128)} %copy-done.14) | copy-start | bytes 245764
  137.7 7.1 %copy-start.17 = (f32[20,8,128]{2,1,0:T(8,128)S(1)}, f32[20,8,128]{2,1,0:T(8,128)}, u32[]{:S(2)}) copy-start(f32[20,8,128]{2,1,0:T(8,128)} %copy-done.16) | copy-start | bytes 245764
  137.7 7.1 %copy-start.19 = (f32[20,8,128]{2,1,0:T(8,128)S(1)}, f32[20,8,128]{2,1,0:T(8,128)}, u32[]{:S(2)}) copy-start(f32[20,8,128]{2,1,0:T(8,128)} %copy-done.18) | copy-start | bytes 245764
  137.7 7.1 %copy-start.47 = (f32[20,8,128]{2,1,0:T(8,128)S(1)}, f32[20,8,128]{2,1,0:T(8,128)}, u32[]{:S(2)}) copy-start(f32[20,8,128]{2,1,0:T(8,128)} %get-tuple-element.436) | copy-start | bytes 245764
  137.8 7.1 %copy-start.48 = (f32[20,8,128]{2,1,0:T(8,128)S(1)}, f32[20,8,128]{2,1,0:T(8,128)}, u32[]{:S(2)}) copy-start(f32[20,8,128]{2,1,0:T(8,128)} %get-tuple-element.438) | copy-start | bytes 245764
  137.8 7.1 %copy-start.49 = (f32[20,8,128]{2,1,0:T(8,128)S(1)}, f32[20,8,128]{2,1,0:T(8,128)}, u32[]{:S(2)}) copy-start(f32[20,8,128]{2,1,0:T(8,128)} %get-tuple-element.440) | copy-start | bytes 245764
  137.8 7.1 %copy-start.68 = (f32[20,8,128]{2,1,0:T(8,128)S(1)}, f32[20,8,128]{2,1,0:T(8,128)}, u32[]{:S(2)}) copy-start(f32[20,8,128]{2,1,0:T(8,128)} %get-tuple-element.253) | copy-start | bytes 245764
  137.8 7.1 %copy-start.73 = (pred[20]{0:T(512)(128)(4,1)S(1)}, pred[20]{0:T(512)(128)(4,1)}, u32[]{:S(2)}) copy-start(pred[20]{0:T(512)(128)(4,1)} %iota_compare_fusion) | copy-start | bytes 64
  138.2 6.6 %collective-permute-start.13 = (f32[19,8,128]{2,1,0:T(8,128)S(1)}, f32[19,8,128]{2,1,0:T(8,128)S(1)}, u32[]{:S(2)}, u32[]{:S(2)}) collective-permute-start(f32[19,8,128]{2,1,0:T(8,128)S(1)} %constant_dynamic-update-slice_fusion.342), channel_id=1, source_target_pairs={{1,0},{2,1},{3,2},{4,3},{5,4},{6,5},{7,6},{8,7},{9,8},{10,9},{11,1... | collective-permute-start | bytes 233480 | tf_op jit(solution)/shard_map/ppermute | solution.py:43
  (57 other events, 61.0 us)
where the time goes:
time: 148 us
  other arithmetic  47.6 us (32%)
  blocking collectives  35 us (24%)
  starting transfers between devices  33 us (22%)
  waiting for transfers between devices  19.3 us (13%)
  between operations  6.77 us (5%)
  local copies, waits for them, and re-layouts  6.04 us (4%)
    psum x1, blocking collectives, drag_seed(): total = lax.psum(partial_drag, 'block')  35 us
    ppermute x12, starting transfers between devices, from_behind(): return lax.ppermute(block, axis, route)  27.5 us
    unnamed x106, other arithmetic  22.5 us
    ppermute x12, waiting for transfers between devices, from_behind(): return lax.ppermute(block, axis, route)  11.8 us
    ppermute x1, starting transfers between devices, padded_2(): lax.ppermute(head, axis, [((i + 1) % count, i) for i in range(count)])  5.5 us
    unnamed x383, local copies, waits for them, and re-layouts  5.14 us
    ppermute x1, waiting for transfers between devices, padded_2(): lax.ppermute(tail, axis, [(i, (i + 1) % count) for i in range(count)])  4.6 us
    broadcast_in_dim x7, other arithmetic, moments(): momentum[coord] = momentum[coord] - state[member]  3.51 us
  transfers between devices with their start and end apart: 14, of which 13 were waited for; matrix products, arithmetic and copies ran while one was open for 3% of the time, Pallas kernels for 0%

commit v1 on v0

v1 whole, which is shorter than its diff:
```python
import functools
import math

import jax
import jax.numpy as jnp
from jax import lax
from jax.experimental import pallas as pl
from jax.experimental.pallas import tpu as pltpu
from jax.sharding import PartitionSpec as P

BX = 4
STEPS = 3
REACH = 2 * STEPS
HALO = STEPS + BX

VELOCITY = (
    (0, 0, 0),
    (1, 0, 0),
    (-1, 0, 0),
    (0, 1, 0),
    (0, -1, 0),
    (0, 0, 1),
    (0, 0, -1),
    (1, 1, 0),
    (-1, -1, 0),
    (1, -1, 0),
    (-1, 1, 0),
    (1, 0, 1),
    (-1, 0, -1),
    (1, 0, -1),
    (-1, 0, 1),
    (0, 1, 1),
    (0, -1, -1),
    (0, 1, -1),
    (0, -1, 1),
)
OPP = (0,) + tuple(m + 1 if m % 2 else m - 1 for m in range(1, 19))
FORCE = 0.02
ROOT_45 = math.sqrt(4.5)
ROOT_2 = math.sqrt(2.0)


def rolled(field, step_y, step_z):
    if step_y:
        field = pltpu.roll(field, step_y % field.shape[0], 0)
    if step_z:
        field = pltpu.roll(field, step_z % field.shape[1], 1)
    return field


def pairs(values):
    plus = [values[2 * k + 1] + values[2 * k + 2] for k in range(9)]
    minus = [values[2 * k + 1] - values[2 * k + 2] for k in range(9)]
    return plus, minus


def first_moments(minus, scale):
    along_x, along_y, along_z = minus[:3]
    if scale != 1.0:
        along_x, along_y, along_z = scale * along_x, scale * along_y, scale * along_z
    along_x = along_x + ((minus[3] + minus[4]) + (minus[5] + minus[6]))
    along_y = along_y + ((minus[3] - minus[4]) + (minus[7] + minus[8]))
    along_z = along_z + ((minus[5] - minus[6]) + (minus[7] - minus[8]))
    return along_x, along_y, along_z


def density_velocity(state):
    plus, minus = pairs(state)
    axes = (plus[0] + plus[1]) + (plus[2] + state[0])
    diagonals = (plus[3] + plus[4]) + (plus[5] + plus[6]) + (plus[7] + plus[8])
    density = axes + diagonals
    inverse = 1.0 / density
    momentum = first_moments(minus, 1.0)
    return density, [part * inverse for part in momentum]


def collide(state, density, flow, open_rate):
    rate = ROOT_45 * open_rate
    x, y, z = (flow[0] + FORCE) * rate, flow[1] * rate, flow[2] * rate
    xx, yy, zz = x * x, y * y, z * z
    base = 1.0 - (xx + yy + zz) * (1.0 / 3.0)
    axis_weight = density * (1.2 / 18.0)
    axis_slope = density * (1.2 * ROOT_2 / 18.0)
    side_weight = density * (1.2 / 36.0)
    side_slope = density * (1.2 * ROOT_2 / 36.0)
    result = [density * 0.4 * base - 0.2 * state[0]]
    for k, along in enumerate((x, y, z, x + y, x - y, x + z, x - z, y + z, y - z)):
        if k < 3:
            even = axis_weight * (base + (xx, yy, zz)[k])
            odd = axis_slope * along
        else:
            even = side_weight * (base + along * along)
            odd = side_slope * along
        result.append((even + odd) - 0.2 * state[2 * k + 1])
        result.append((even - odd) - 0.2 * state[2 * k + 2])
    return result


def spread(level, slope):
    x, y, z = slope
    result = [level]
    for along in (x, y, z, x + y, x - y, x + z, x - z, y + z, y - z):
        result.append(level + along)
        result.append(level - along)
    return result


def pull(source, plane, word):
    here = [source[m, plane] for m in range(19)]
    result = [here[0]]
    for m in range(1, 19):
        step_x, step_y, step_z = VELOCITY[m]
        moved = here[m] if step_x == 0 else source[m, plane - step_x]
        moved = rolled(moved, step_y, step_z)
        result.append(jnp.where((word & (1 << m)) != 0, moved, here[OPP[m]]))
    return result


def link_word(behind, here, ahead):
    rows = lax.broadcasted_iota(jnp.int32, here.shape, 0)
    columns = lax.broadcasted_iota(jnp.int32, here.shape, 1)
    joined = behind + 2 * here + 4 * ahead
    word = jnp.zeros_like(here)
    for step_y in (-1, 0, 1):
        for step_z in (-1, 0, 1):
            if step_y and step_z:
                inner = {0: 1}
            else:
                inner = {1: 0, 0: 1, -1: 2}
            near = rolled(joined, step_y, step_z)
            if step_y == 1:
                near = jnp.where(rows == 0, 0, near)
            if step_y == -1:
                near = jnp.where(rows == here.shape[0] - 1, 0, near)
            if step_z == 1:
                near = jnp.where(columns == 0, 0, near)
            if step_z == -1:
                near = jnp.where(columns == here.shape[1] - 1, 0, near)
            for step_x, place in inner.items():
                if (step_x, step_y, step_z) == (0, 0, 0):
                    continue
                m = VELOCITY.index((step_x, step_y, step_z))
                word = word | ((near & (1 << place)) << (m - place))
    return jnp.where(here > 0, word, 0)


def each_plane(low, high, body):
    def two(index, carry):
        body(low + 2 * index)
        body(low + 2 * index + 1)
        return carry

    lax.fori_loop(0, (high - low) // 2, two, 0)
    if (high - low) % 2:
        body(high - 1)


def forward_kernel(
    home, pops, marked, left, right, final, history, opens, words, drag, first, even, odd, fluid, sems
):
    total = home + 2 * HALO
    copies = [
        pltpu.make_async_copy(pops, first.at[pl.ds(0, 19), pl.ds(HALO, home)], sems.at[0]),
        pltpu.make_async_copy(marked, first.at[19, pl.ds(HALO, home)], sems.at[1]),
        pltpu.make_async_copy(left, first.at[:, pl.ds(0, HALO)], sems.at[2]),
        pltpu.make_async_copy(right, first.at[:, pl.ds(HALO + home, HALO)], sems.at[3]),
    ]
    for copy in copies:
        copy.start()
    for copy in copies:
        copy.wait()

    def remember(step, plane, density, flow):
        history[4 * step, plane] = density
        for axis in range(3):
            history[4 * step + 1 + axis, plane] = flow[axis]

    def start(plane):
        mark = first[19, plane]
        fluid[plane] = (mark >= 0.0).astype(jnp.int32)
        design = jnp.maximum(mark, 0.0)
        open_rate = (1.0 + 4.0 * design) / (1.6 + 3.4 * design)
        opens[plane] = open_rate
        state = [first[m, plane] for m in range(19)]
        density, flow = density_velocity(state)
        remember(0, plane, density, flow)
        for m, part in enumerate(collide(state, density, flow, open_rate)):
            even[m, plane] = part

    each_plane(0, total, start)

    def link(plane):
        words[plane] = link_word(fluid[plane - 1], fluid[plane], fluid[plane + 1])

    each_plane(1, total - 1, link)

    def advance(step, source, target, plane):
        state = pull(source, plane, words[plane])
        density, flow = density_velocity(state)
        remember(step, plane, density, flow)
        for m, part in enumerate(collide(state, density, flow, opens[plane])):
            target[m, plane] = part

    each_plane(1, total - 1, functools.partial(advance, 1, even, odd))
    each_plane(2, total - 2, functools.partial(advance, 2, odd, even))

    drag[...] = jnp.zeros_like(drag)

    def finish(plane):
        state = pull(even, plane, words[plane])
        density, flow = density_velocity(state)
        remember(3, plane, density, flow)
        is_fluid = fluid[plane] > 0
        for m in range(19):
            final[m, plane - STEPS] = jnp.where(is_fluid, state[m], first[m, plane])
        square = flow[0] * flow[0] + flow[1] * flow[1] + flow[2] * flow[2]
        own = (plane >= HALO) & (plane < HALO + home)
        drag[...] += jnp.where(is_fluid & own, square / opens[plane], 0.0)

    each_plane(STEPS, total - STEPS, finish)


def backward_kernel(home, history, opens, words, marked, gradient, even, odd, share):
    def recall(step, plane):
        return history[4 * step, plane], [history[4 * step + 1 + axis, plane] for axis in range(3)]

    def seed(plane):
        density, flow = recall(STEPS, plane)
        damping = 1.0 / opens[plane]
        square = flow[0] * flow[0] + flow[1] * flow[1] + flow[2] * flow[2]
        share[plane] = -square * damping
        factor = 2.0 * damping / density
        slope = [part * factor for part in flow]
        values = spread(-square * factor, slope)
        for m in range(19):
            even[OPP[m], plane] = values[m]

    each_plane(HALO - STEPS, HALO + home + STEPS, seed)

    def retreat(step, source, target, plane):
        mirrored = pull(source, plane, words[plane])
        adjoint = [mirrored[OPP[m]] for m in range(19)]
        density, flow = recall(step, plane)
        open_rate = opens[plane]
        force_flow = [flow[0] + FORCE, flow[1], flow[2]]
        x, y, z = [open_rate * part for part in force_flow]
        plus, minus = pairs(adjoint)
        mx, my, mz = [part * (1.0 / 12.0) for part in first_moments(minus, 2.0)]
        xy_plus, xz_plus, yz_plus = plus[3] + plus[4], plus[5] + plus[6], plus[7] + plus[8]
        axes = [2.0 * plus[k] for k in range(3)]
        whole = 12.0 * adjoint[0] + (axes[0] + axes[1] + axes[2]) + (xy_plus + xz_plus + yz_plus)
        third = whole * (1.0 / 3.0)
        xx = axes[0] + (xy_plus + xz_plus) - third
        yy = axes[1] + (xy_plus + yz_plus) - third
        zz = axes[2] + (xz_plus + yz_plus) - third
        xy, xz, yz = plus[3] - plus[4], plus[5] - plus[6], plus[7] - plus[8]
        hx = 0.25 * (xx * x + xy * y + xz * z)
        hy = 0.25 * (xy * x + yy * y + yz * z)
        hz = 0.25 * (xz * x + yz * y + zz * z)
        rate = 1.2 * open_rate
        slope = [rate * (mx + hx), rate * (my + hy), rate * (mz + hz)]
        pushed = slope[0] * force_flow[0] + slope[1] * force_flow[1] + slope[2] * force_flow[2]
        share[plane] += density * pushed
        if target is None:
            return
        level = whole * (1.2 / 36.0) + 1.2 * (
            x * (mx + 0.5 * hx) + y * (my + 0.5 * hy) + z * (mz + 0.5 * hz)
        )
        level = level - (slope[0] * flow[0] + slope[1] * flow[1] + slope[2] * flow[2])
        values = spread(level, slope)
        for m in range(19):
            target[OPP[m], plane] = values[m] - 0.2 * adjoint[m]

    each_plane(HALO - 2, HALO + home + 2, functools.partial(retreat, 2, even, odd))
    each_plane(HALO - 1, HALO + home + 1, functools.partial(retreat, 1, odd, even))
    each_plane(HALO, HALO + home, functools.partial(retreat, 0, even, None))

    def close(plane):
        design = marked[plane]
        slope = 3.0 / ((1.6 + 3.4 * design) * (1.0 + 4.0 * design))
        gradient[plane] = jnp.where(design >= 0.0, share[plane + HALO] * slope, 0.0)

    each_plane(0, home, close)


def place_kernel(blocks, reach, where, source, out, zeros, sems):
    zeros[...] = jnp.zeros_like(zeros)
    most = source.shape[1] // BX - 1
    for slot in range(blocks):
        target = out.at[:, pl.ds(slot * BX, BX)]
        live = slot < where[1]
        begin = jnp.clip(where[0] + reach + slot, 0, most) * BX

        @pl.when(live)
        def _():
            pltpu.make_async_copy(source.at[:, pl.ds(begin, BX)], target, sems.at[slot]).start()

        @pl.when(jnp.logical_not(live))
        def _():
            pltpu.make_async_copy(zeros, target, sems.at[slot]).start()

    for slot in range(blocks):
        target = out.at[:, pl.ds(slot * BX, BX)]
        pltpu.make_async_copy(zeros, target, sems.at[slot]).wait()


def place(source, where, blocks, reach):
    members = source.shape[0]
    tail = source.shape[2:]
    return pl.pallas_call(
        functools.partial(place_kernel, blocks, reach),
        out_shape=jax.ShapeDtypeStruct((members, blocks * BX) + tail, jnp.float32),
        in_specs=[pl.BlockSpec(memory_space=pltpu.SMEM), pl.BlockSpec(memory_space=pl.ANY)],
        out_specs=pl.BlockSpec(memory_space=pl.ANY),
        scratch_shapes=[
            pltpu.VMEM((members, BX) + tail, jnp.float32),
            pltpu.SemaphoreType.DMA((blocks,)),
        ],
        cost_estimate=pl.CostEstimate(flops=0, bytes_accessed=3_200_000, transcendentals=0),
        name="place_populations",
    )(where, source)


def scale_kernel(home, cells, where, drag, left, own, right, out, joined):
    joined[pl.ds(0, home)] = left[...]
    joined[pl.ds(home, home)] = own[...]
    joined[pl.ds(2 * home, home)] = right[...]
    factor = cells / jnp.sum(drag[...])
    for plane in range(out.shape[0]):
        spot = jnp.clip(where[0] * BX + home + plane, 0, 3 * home - 1)
        live = plane < where[1] * BX
        out[plane] = jnp.where(live, joined[spot] * factor, 0.0)


def body(populations, design, fluid_mask, owner_after):
    count = lax.axis_size("block")
    rank = lax.axis_index("block")
    home, width_y, width_z = design.shape
    home_blocks = home // BX
    slots = home_blocks + 2
    total = home + 2 * HALO
    plane = (width_y, width_z)
    f32 = jnp.float32
    vmem = pl.BlockSpec(memory_space=pltpu.VMEM)
    anywhere = pl.BlockSpec(memory_space=pl.ANY)
    smem = pl.BlockSpec(memory_space=pltpu.SMEM)
    up = [(i, (i + 1) % count) for i in range(count)]
    down = [((i + 1) % count, i) for i in range(count)]

    marked = jnp.where(fluid_mask > 0, design, -1.0)
    tail = jnp.concatenate([populations[:, home - HALO :], marked[None, home - HALO :]], axis=0)
    head = jnp.concatenate([populations[:, :HALO], marked[None, :HALO]], axis=0)
    left = lax.ppermute(tail, "block", up)
    right = lax.ppermute(head, "block", down)

    members = jnp.arange(count + 1, dtype=jnp.int32)
    starts = jnp.sum((owner_after[None, :] < members[:, None]).astype(jnp.int32), axis=1)
    shifts = starts - home_blocks * members
    far = jnp.any(jnp.abs(shifts) > 1)
    begin = lax.dynamic_index_in_dim(shifts, rank, 0, keepdims=False)
    after = lax.dynamic_index_in_dim(shifts, rank + 1, 0, keepdims=False)
    where = jnp.stack([begin, after + home_blocks - begin])

    final, history, opens, words, drag = pl.pallas_call(
        functools.partial(forward_kernel, home),
        out_shape=[
            jax.ShapeDtypeStruct((19, home + 2 * BX) + plane, f32),
            jax.ShapeDtypeStruct((4 * (STEPS + 1), total) + plane, f32),
            jax.ShapeDtypeStruct((total,) + plane, f32),
            jax.ShapeDtypeStruct((total,) + plane, jnp.int32),
            jax.ShapeDtypeStruct(plane, f32),
        ],
        in_specs=[anywhere] * 4,
        out_specs=[vmem] * 5,
        scratch_shapes=[
            pltpu.VMEM((20, total) + plane, f32),
            pltpu.VMEM((19, total) + plane, f32),
            pltpu.VMEM((19, total) + plane, f32),
            pltpu.VMEM((total,) + plane, jnp.int32),
            pltpu.SemaphoreType.DMA((4,)),
        ],
        compiler_params=pltpu.CompilerParams(vmem_limit_bytes=24 * 2**20),
        cost_estimate=pl.CostEstimate(flops=25_000_000, bytes_accessed=6_000_000, transcendentals=0),
        name="forward_steps",
    )(populations, marked, left, right)

    distance = 1
    while distance < count:
        swap = [(i, i ^ distance) for i in range(count)]
        drag = drag + lax.ppermute(drag, "block", swap)
        distance *= 2

    gradient = pl.pallas_call(
        functools.partial(backward_kernel, home),
        out_shape=jax.ShapeDtypeStruct((home,) + plane, f32),
        in_specs=[vmem] * 4,
        out_specs=vmem,
        scratch_shapes=[
            pltpu.VMEM((19, total) + plane, f32),
            pltpu.VMEM((19, total) + plane, f32),
            pltpu.VMEM((total,) + plane, f32),
        ],
        compiler_params=pltpu.CompilerParams(vmem_limit_bytes=24 * 2**20),
        cost_estimate=pl.CostEstimate(flops=15_000_000, bytes_accessed=4_000_000, transcendentals=0),
        name="backward_steps",
    )(history, opens, words, marked)

    gradient_left = lax.ppermute(gradient, "block", up[:-1])
    gradient_right = lax.ppermute(gradient, "block", down[:-1])
    cells = float(count * home * width_y * width_z)
    sensitivity = pl.pallas_call(
        functools.partial(scale_kernel, home, cells),
        out_shape=jax.ShapeDtypeStruct((slots * BX,) + plane, f32),
        in_specs=[smem] + [vmem] * 4,
        out_specs=vmem,
        scratch_shapes=[pltpu.VMEM((3 * home,) + plane, f32)],
        name="place_gradient",
    )(where, drag, gradient_left, gradient, gradient_right)

    def by_one(kept):
        return place(kept, where, slots, 1)

    def by_more(kept):
        own = kept[:, BX : BX + home]
        before = lax.ppermute(own, "block", up[:-1])
        behind = lax.ppermute(own, "block", down[:-1])
        return place(jnp.concatenate([before, own, behind], axis=1), where, slots, home_blocks)

    populations_after = lax.cond(far, by_more, by_one, final)
    return (populations_after, sensitivity)


def solution(mesh):
    placed = (
        P(None, ("group", "block"), None, None),
        P(("group", "block"), None, None),
        P(("group", "block"), None, None),
        P("group"),
    )
    return jax.shard_map(
        body,
        mesh=mesh,
        in_specs=placed,
        out_specs=(P(None, ("group", "block"), None, None), P(("group", "block"), None, None)),
        check_vma=False,
    )
```

time: 148 us -> 53.2 us (0.36)
  other arithmetic: 47.6 us -> 3 us
  blocking collectives: 35 us -> 0 us
  starting transfers between devices: 33 us -> 18.8 us
  Pallas kernels: 0 us -> 13.5 us
  waiting for transfers between devices: 19.3 us -> 11.6 us
  between operations: 6.77 us -> 2.66 us
  local copies, waits for them, and re-layouts: 6.04 us -> 3.21 us
    psum x1 -> x0, blocking collectives: 35 us -> none  [drag_seed(): total = lax.psum(partial_drag, 'block')]
    unnamed x106 -> x0, other arithmetic: 22.5 us -> none
    ppermute x14 -> x8, starting transfers between devices: 33 us -> 18.8 us  [the longest x4 8.93 us: body(): drag = drag + lax.ppermute(drag, 'block', swap)]
    pallas_call x0 -> x4, Pallas kernels: none -> 13.5 us  [the longest x1 7.29 us: body(): pl.pallas_call(functools.partial(forward_kernel, home), out_shape=[jax.Sh...]
    broadcast_in_dim x22 -> x0, other arithmetic: 7.82 us -> none  [the longest x7 3.51 us: moments(): momentum[coord] = momentum[coord] - state[member]]
    ppermute x14 -> x8, waiting for transfers between devices: 19.3 us -> 11.6 us  [the longest x1 7.38 us: body(): left = lax.ppermute(tail, 'block', up)]
    mul x9 -> x0, other arithmetic: 4.11 us -> none  [the longest x1 2.81 us: body(): return (final, gradient * live)]
    unnamed x383 -> x12, local copies, waits for them, and re-layouts: 5.14 us -> 1.24 us
  transfers between devices with their start and end apart: 14 -> 8, of which waited for: 13 -> 3; matrix products, arithmetic and copies ran while one was open for 3% -> 5% of each run, Pallas kernels for 0% -> 9%
where the time goes in v1:
time: 53.2 us; the launch traced here: 52.8 us
  starting transfers between devices  18.8 us (35%)
  Pallas kernels  13.5 us (25%)
  waiting for transfers between devices  11.6 us (22%)
  local copies, waits for them, and re-layouts  3.21 us (6%)
  other arithmetic  3 us (6%)
  between operations  2.66 us (5%)
    ppermute x4, starting transfers between devices, body(): drag = drag + lax.ppermute(drag, 'block', swap)  8.93 us
    ppermute x1, waiting for transfers between devices, body(): left = lax.ppermute(tail, 'block', up)  7.38 us
    pallas_call x1, Pallas kernels, body(): pl.pallas_call(functools.partial(forward_kernel, home), out_shape=[jax.Sh...  7.29 us
    ppermute x1, starting transfers between devices, body(): right = lax.ppermute(head, 'block', down)  5.06 us
    ppermute x4, waiting for transfers between devices, body(): drag = drag + lax.ppermute(drag, 'block', swap)  4.18 us
    ppermute x1, starting transfers between devices, body(): gradient_left = lax.ppermute(gradient, 'block', up[:-1])  3.03 us
    pallas_call x1, Pallas kernels, body(): pl.pallas_call(functools.partial(backward_kernel, home), out_shape=jax.Sh...  2.86 us
    pallas_call x1, Pallas kernels, body(): pl.pallas_call(functools.partial(scale_kernel, home, cells), out_shape=ja...  1.67 us
  transfers between devices with their start and end apart: 8, of which 3 were waited for; matrix products, arithmetic and copies ran while one was open for 5% of the time, Pallas kernels for 9%

profile of v1, /device:TPU:0, one launch (start us, length us, event | category | flops | bytes accessed | tf_op | source)
XLA Modules:
  0.0 52.8 jit_solution(16648527602834929281)
XLA Ops:
  0.6 0.0 copy-start
  0.6 0.9 %compare_select_fusion.marked = f32[12,8,128]{2,1,0:T(8,128)S(1)} fusion(f32[12,8,128]{2,1,0:T(8,128)} %param.7, s32[12,8,128]{2,1,0:T(8,128)} %param.8), kind=kLoop, calls=%fused_computation.3 | loop fusion | flops 24576 | bytes 147456 | tf_op jit(solution)/shard_map/jit(_where)/select_n | solution.py:350
  1.6 0.0 copy-start.5
  1.6 1.3 %fusion = (f32[19,7,8,128]{3,2,1,0:T(8,128)S(1)}, f32[19,7,8,128]{3,2,1,0:T(8,128)S(1)}) fusion(f32[19,12,8,128]{3,2,1,0:T(8,128)} %pops.1), kind=kLoop, calls=%fused_computation.11 | loop fusion | bytes 2179072 | tf_op jit(solution)/shard_map/slice | solution.py:352
  2.9 0.5 collective-permute-start.2
  3.5 5.1 %collective-permute-start.3 = (f32[20,7,8,128]{3,2,1,0:T(8,128)S(1)}, f32[20,7,8,128]{3,2,1,0:T(8,128)S(1)}, u32[]{:S(2)}, u32[]{:S(2)}) collective-permute-start(f32[20,7,8,128]{3,2,1,0:T(8,128)S(1)} %pad_maximum_fusion.2), channel_id=1, source_target_pairs={{1,0},{2,1},{3,2},{4,3},{5,4},{6,5},{7,6},{8,7},{9,8},{10,9},{11,1... | collective-permute-start | bytes 1720328 | tf_op jit(solution)/shard_map/ppermute | solution.py:354
  8.5 7.4 %collective-permute-done.2.left = f32[20,7,8,128]{3,2,1,0:T(8,128)S(1)} collective-permute-done((f32[20,7,8,128]{3,2,1,0:T(8,128)S(1)}, f32[20,7,8,128]{3,2,1,0:T(8,128)S(1)}, u32[]{:S(2)}, u32[]{:S(2)}) %collective-permute-start.2) | collective-permute-done | bytes 573472 | tf_op jit(solution)/shard_map/ppermute | solution.py:353
  15.9 0.0 collective-permute-done.3.right
  15.9 7.3 %forward_steps.1 = (f32[19,20,8,128]{3,2,1,0:T(8,128)}, f32[16,26,8,128]{3,2,1,0:T(8,128)S(1)}, f32[26,8,128]{2,1,0:T(8,128)S(1)}, s32[26,8,128]{2,1,0:T(8,128)S(1)}, f32[8,128]{1,0:T(8,128)S(1)}) custom-call(f32[19,12,8,128]{3,2,1,0:T(8,128)S(1)} %copy-done, f32[12,8,128]{2,1,0:T(8,128)S(1)} %compare_select_fusion.marked, ...), custom_call_target="tpu_custom_call" | custom-call | flops 25000000 | bytes 6000000 | tf_op jit(solution)/shard_map/forward_steps/pallas_call | solution.py:364
  23.2 5.6 %collective-permute-start.4 = (f32[8,128]{1,0:T(8,128)S(1)}, f32[8,128]{1,0:T(8,128)S(1)}, u32[]{:S(2)}, u32[]{:S(2)}) collective-permute-start(f32[8,128]{1,0:T(8,128)S(1)} %get-tuple-element.23), channel_id=1, source_target_pairs={{0,1},{1,0},{2,3},{3,2},{4,5},{5,4},{6,7},{7,6},{8,9},{9,8},{10,11... | collective-permute-start | bytes 12296 | tf_op jit(solution)/shard_map/ppermute | solution.py:390
  28.8 0.1 convert_reduce_fusion
  28.9 0.7 %collective-permute-done.4 = f32[8,128]{1,0:T(8,128)S(1)} collective-permute-done((f32[8,128]{1,0:T(8,128)S(1)}, f32[8,128]{1,0:T(8,128)S(1)}, u32[]{:S(2)}, u32[]{:S(2)}) %collective-permute-start.4) | collective-permute-done | bytes 4128 | tf_op jit(solution)/shard_map/ppermute | solution.py:390
  29.6 0.1 collective-permute-start.5
  29.8 3.5 %collective-permute-done.5 = f32[8,128]{1,0:T(8,128)S(1)} collective-permute-done((f32[8,128]{1,0:T(8,128)S(1)}, f32[8,128]{1,0:T(8,128)S(1)}, u32[]{:S(2)}, u32[]{:S(2)}) %collective-permute-start.5) | collective-permute-done | bytes 4128 | tf_op jit(solution)/shard_map/ppermute | solution.py:390
  33.2 0.6 %collective-permute-start.6 = (f32[8,128]{1,0:T(8,128)S(1)}, f32[8,128]{1,0:T(8,128)S(1)}, u32[]{:S(2)}, u32[]{:S(2)}) collective-permute-start(f32[8,128]{1,0:T(8,128)S(1)} %add.33), channel_id=1, source_target_pairs={{0,4},{1,5},{2,6},{3,7},{4,0},{5,1},{6,2},{7,3},{8,12},{9,13},{10,... | collective-permute-start | bytes 12296 | tf_op jit(solution)/shard_map/ppermute | solution.py:390
  33.8 0.6 %compare_reduce_fusion = pred[]{:T(512)} fusion(s32[17]{0:T(128)S(1)} %convert_reduce_fusion), kind=kLoop, calls=%fused_computation.8 | loop fusion | flops 84 | bytes 69 | tf_op jit(solution)/shard_map/reduce_or | solution.py:359
  34.4 0.7 %fusion.1 = (s32[1]{0:T(128)}, s32[1]{0:T(128)}) fusion(s32[17]{0:T(128)S(1)} %multiply_subtract_fusion, s32[]{:T(128)S(6)} %select_n.11, s32[]{:T(128)S(6)} %select_n.12), kind=kLoop, calls=%fused_computation.12 | loop fusion | bytes 24 | tf_op jit(solution)/shard_map/jit(dynamic_index_in_dim)/dynamic_slice | solution.py:360
  36.3 2.9 %backward_steps.1.own = f32[12,8,128]{2,1,0:T(8,128)S(1)} custom-call(f32[16,26,8,128]{3,2,1,0:T(8,128)S(1)} %get-tuple-element.24.history, f32[26,8,128]{2,1,0:T(8,128)S(1)} %get-tuple-element.25.opens, s32[26,8,128]{2,1,0:T(8,128)S(1)} %get-tuple-element.26.words, f32[12,8,128]{2,1,0:T(8,128)S(1)} %compare_select_fusion.marked), custom_call_target="tpu_custom_call" | custom-call | flops 15000000 | bytes 4000000 | tf_op jit(solution)/shard_map/backward_steps/pallas_call | solution.py:393
  39.2 1.3 %collective-permute-start.9 = (f32[12,8,128]{2,1,0:T(8,128)S(1)}, f32[12,8,128]{2,1,0:T(8,128)S(1)}, u32[]{:S(2)}, u32[]{:S(2)}) collective-permute-start(f32[12,8,128]{2,1,0:T(8,128)S(1)} %backward_steps.1.own), channel_id=1, source_target_pairs={{1,0},{2,1},{3,2},{4,3},{5,4},{6,5},{7,6},{8,7},{9,8},{10,9},{11,1... | collective-permute-start | bytes 147464 | tf_op jit(solution)/shard_map/ppermute | solution.py:409
  40.5 3.0 %collective-permute-start.8 = (f32[12,8,128]{2,1,0:T(8,128)S(1)}, f32[12,8,128]{2,1,0:T(8,128)S(1)}, u32[]{:S(2)}, u32[]{:S(2)}) collective-permute-start(f32[12,8,128]{2,1,0:T(8,128)S(1)} %backward_steps.1.own), channel_id=1, source_target_pairs={{0,1},{1,2},{2,3},{3,4},{4,5},{5,6},{6,7},{7,8},{8,9},{9,10},{10,1... | collective-permute-start | bytes 147464 | tf_op jit(solution)/shard_map/ppermute | solution.py:408
  43.6 0.0 collective-permute-done.6
  43.6 2.7 %collective-permute-start.7 = (f32[8,128]{1,0:T(8,128)S(1)}, f32[8,128]{1,0:T(8,128)S(1)}, u32[]{:S(2)}, u32[]{:S(2)}) collective-permute-start(f32[8,128]{1,0:T(8,128)S(1)} %add.34), channel_id=1, source_target_pairs={{0,8},{1,9},{2,10},{3,11},{4,12},{5,13},{6,14},{7,15},{8,0},{9,1},... | collective-permute-start | bytes 12296 | tf_op jit(solution)/shard_map/ppermute | solution.py:390
  46.2 0.6 %pad_add_fusion.where = s32[2]{0:T(128)S(1)} fusion(s32[1]{0:T(128)S(6)} %sub.8, s32[1]{0:T(128)} %get-tuple-element.31), kind=kLoop, calls=%fused_computation.9 | loop fusion | flops 2 | bytes 16 | tf_op jit(solution)/shard_map/stack | solution.py:362
  47.5 1.7 %conditional.1 = (f32[19,20,8,128]{3,2,1,0:T(8,128)S(1)}) conditional(s32[]{:T(128)} %convert_element_type.7, (s32[2]{0:T(128)S(1)}, f32[19,20,8,128]{3,2,1,0:T(8,128)}) %tuple.14, (f32[19,20,8,128]{3,2,1,0:T(8,128)}, s32[2]{0:T(128)S(1)}) %tuple.15), branch_computations={%region_2.3_spmd, %region_3.4_spmd} | conditional | flops 1400832 | bytes 18142296 | solution.py:429
  47.5 1.7 %place_populations.2 = f32[19,20,8,128]{3,2,1,0:T(8,128)S(1)} custom-call(s32[2]{0:T(128)S(1)} %get-tuple-element.8.where, f32[19,20,8,128]{3,2,1,0:T(8,128)} %get-tuple-element.12.source), custom_call_target="tpu_custom_call" | custom-call | bytes 3200000 | tf_op jit(solution)/shard_map/cond/branch_0_fun/place_populations/pallas_call | solution.py:310
  49.2 0.0 copy-start.2
  49.2 0.0 collective-permute-done.7
  49.2 0.6 %add.35.drag = f32[8,128]{1,0:T(8,128)} add(f32[8,128]{1,0:T(8,128)S(1)} %add.34, f32[8,128]{1,0:T(8,128)S(1)} %collective-permute-done.7) | non-fusion elementwise | flops 1024 | bytes 12288 | tf_op jit(solution)/shard_map/add | solution.py:390
  49.9 0.0 collective-permute-done.8.left
  49.9 0.6 %copy-done.3 = f32[12,8,128]{2,1,0:T(8,128)} copy-done((f32[12,8,128]{2,1,0:T(8,128)}, f32[12,8,128]{2,1,0:T(8,128)S(1)}, u32[]{:S(2)}) %copy-start.3) | copy-done | bytes 49176
  50.5 0.6 %copy-done.4 = f32[12,8,128]{2,1,0:T(8,128)} copy-done((f32[12,8,128]{2,1,0:T(8,128)}, f32[12,8,128]{2,1,0:T(8,128)S(1)}, u32[]{:S(2)}) %copy-start.4) | copy-done | bytes 49176
  51.1 1.7 %place_gradient.1 = f32[20,8,128]{2,1,0:T(8,128)} custom-call(s32[2]{0:T(128)S(1)} %pad_add_fusion.where, f32[8,128]{1,0:T(8,128)} %add.35.drag, f32[12,8,128]{2,1,0:T(8,128)} %copy-done.4, f32[12,8,128]{2,1,0:T(8,128)} %copy-done.1, f32[12,8,128]{2,1,0:T(8,128)} %copy-done.3), custom_call_target="tpu_custom_call" | custom-call | tf_op jit(solution)/shard_map/place_gradient/pallas_call | solution.py:411
  (15 shorter events, 0.1 us)
Async XLA Ops:
  0.6 15.3 %copy-start = (f32[19,12,8,128]{3,2,1,0:T(8,128)S(1)}, f32[19,12,8,128]{3,2,1,0:T(8,128)}, u32[]{:S(2)}) copy-start(f32[19,12,8,128]{3,2,1,0:T(8,128)} %pops.1) | copy-start | bytes 2801668
  1.6 27.2 %copy-start.5 = (s32[48]{0:T(128)S(1)}, s32[48]{0:T(128)}, u32[]{:S(2)}) copy-start(s32[48]{0:T(128)} %param.9) | copy-start | bytes 580
  2.9 13.0 %collective-permute-start.2 = (f32[20,7,8,128]{3,2,1,0:T(8,128)S(1)}, f32[20,7,8,128]{3,2,1,0:T(8,128)S(1)}, u32[]{:S(2)}, u32[]{:S(2)}) collective-permute-start(f32[20,7,8,128]{3,2,1,0:T(8,128)S(1)} %pad_maximum_fusion.1), channel_id=1, source_target_pairs={{0,1},{1,2},{2,3},{3,4},{4,5},{5,6},{6,7},{7,8},{8,9},{9,10},{10,1... | collective-permute-start | bytes 1720328 | tf_op jit(solution)/shard_map/ppermute | solution.py:353
  3.5 12.5 %collective-permute-start.3 = (f32[20,7,8,128]{3,2,1,0:T(8,128)S(1)}, f32[20,7,8,128]{3,2,1,0:T(8,128)S(1)}, u32[]{:S(2)}, u32[]{:S(2)}) collective-permute-start(f32[20,7,8,128]{3,2,1,0:T(8,128)S(1)} %pad_maximum_fusion.2), channel_id=1, source_target_pairs={{1,0},{2,1},{3,2},{4,3},{5,4},{6,5},{7,6},{8,7},{9,8},{10,9},{11,1... | collective-permute-start | bytes 1720328 | tf_op jit(solution)/shard_map/ppermute | solution.py:354
  23.2 6.4 %collective-permute-start.4 = (f32[8,128]{1,0:T(8,128)S(1)}, f32[8,128]{1,0:T(8,128)S(1)}, u32[]{:S(2)}, u32[]{:S(2)}) collective-permute-start(f32[8,128]{1,0:T(8,128)S(1)} %get-tuple-element.23), channel_id=1, source_target_pairs={{0,1},{1,0},{2,3},{3,2},{4,5},{5,4},{6,7},{7,6},{8,9},{9,8},{10,11... | collective-permute-start | bytes 12296 | tf_op jit(solution)/shard_map/ppermute | solution.py:390
  29.6 3.6 %collective-permute-start.5 = (f32[8,128]{1,0:T(8,128)S(1)}, f32[8,128]{1,0:T(8,128)S(1)}, u32[]{:S(2)}, u32[]{:S(2)}) collective-permute-start(f32[8,128]{1,0:T(8,128)S(1)} %add.32), channel_id=1, source_target_pairs={{0,2},{1,3},{2,0},{3,1},{4,6},{5,7},{6,4},{7,5},{8,10},{9,11},{10,... | collective-permute-start | bytes 12296 | tf_op jit(solution)/shard_map/ppermute | solution.py:390
  33.2 10.3 %collective-permute-start.6 = (f32[8,128]{1,0:T(8,128)S(1)}, f32[8,128]{1,0:T(8,128)S(1)}, u32[]{:S(2)}, u32[]{:S(2)}) collective-permute-start(f32[8,128]{1,0:T(8,128)S(1)} %add.33), channel_id=1, source_target_pairs={{0,4},{1,5},{2,6},{3,7},{4,0},{5,1},{6,2},{7,3},{8,12},{9,13},{10,... | collective-permute-start | bytes 12296 | tf_op jit(solution)/shard_map/ppermute | solution.py:390
  39.2 8.3 %copy-start.1 = (f32[12,8,128]{2,1,0:T(8,128)}, f32[12,8,128]{2,1,0:T(8,128)S(1)}, u32[]{:S(2)}) copy-start(f32[12,8,128]{2,1,0:T(8,128)S(1)} %backward_steps.1.own) | copy-start | bytes 147460
  39.2 10.7 %collective-permute-start.9 = (f32[12,8,128]{2,1,0:T(8,128)S(1)}, f32[12,8,128]{2,1,0:T(8,128)S(1)}, u32[]{:S(2)}, u32[]{:S(2)}) collective-permute-start(f32[12,8,128]{2,1,0:T(8,128)S(1)} %backward_steps.1.own), channel_id=1, source_target_pairs={{1,0},{2,1},{3,2},{4,3},{5,4},{6,5},{7,6},{8,7},{9,8},{10,9},{11,1... | collective-permute-start | bytes 147464 | tf_op jit(solution)/shard_map/ppermute | solution.py:409
  40.5 9.4 %collective-permute-start.8 = (f32[12,8,128]{2,1,0:T(8,128)S(1)}, f32[12,8,128]{2,1,0:T(8,128)S(1)}, u32[]{:S(2)}, u32[]{:S(2)}) collective-permute-start(f32[12,8,128]{2,1,0:T(8,128)S(1)} %backward_steps.1.own), channel_id=1, source_target_pairs={{0,1},{1,2},{2,3},{3,4},{4,5},{5,6},{6,7},{7,8},{8,9},{9,10},{10,1... | collective-permute-start | bytes 147464 | tf_op jit(solution)/shard_map/ppermute | solution.py:408
  43.6 5.6 %collective-permute-start.7 = (f32[8,128]{1,0:T(8,128)S(1)}, f32[8,128]{1,0:T(8,128)S(1)}, u32[]{:S(2)}, u32[]{:S(2)}) collective-permute-start(f32[8,128]{1,0:T(8,128)S(1)} %add.34), channel_id=1, source_target_pairs={{0,8},{1,9},{2,10},{3,11},{4,12},{5,13},{6,14},{7,15},{8,0},{9,1},... | collective-permute-start | bytes 12296 | tf_op jit(solution)/shard_map/ppermute | solution.py:390
  49.2 3.6 %copy-start.2 = (f32[19,20,8,128]{3,2,1,0:T(8,128)}, f32[19,20,8,128]{3,2,1,0:T(8,128)S(1)}, u32[]{:S(2)}) copy-start(f32[19,20,8,128]{3,2,1,0:T(8,128)S(1)} %get-tuple-element.33) | copy-start | bytes 4669444
  49.9 0.6 %copy-start.3 = (f32[12,8,128]{2,1,0:T(8,128)}, f32[12,8,128]{2,1,0:T(8,128)S(1)}, u32[]{:S(2)}) copy-start(f32[12,8,128]{2,1,0:T(8,128)S(1)} %collective-permute-done.9.right) | copy-start | bytes 147460
  50.5 0.6 %copy-start.4 = (f32[12,8,128]{2,1,0:T(8,128)}, f32[12,8,128]{2,1,0:T(8,128)S(1)}, u32[]{:S(2)}) copy-start(f32[12,8,128]{2,1,0:T(8,128)S(1)} %collective-permute-done.8.left) | copy-start | bytes 147460

commit v2 on v1

--- a/solution.py
+++ b/solution.py
@@ -384,11 +384,7 @@
         name="forward_steps",
     )(populations, marked, left, right)
 
-    distance = 1
-    while distance < count:
-        swap = [(i, i ^ distance) for i in range(count)]
-        drag = drag + lax.ppermute(drag, "block", swap)
-        distance *= 2
+    drag = lax.all_gather(drag, "block")
 
     gradient = pl.pallas_call(
         functools.partial(backward_kernel, home),

time: 53.2 us -> 63.4 us (1.19)
  blocking collectives: 0 us -> 22.2 us
  waiting for transfers between devices: 11.6 us -> 4.82 us
  starting transfers between devices: 18.8 us -> 14.9 us
  local copies, waits for them, and re-layouts: 3.21 us -> 2.55 us
    all_gather x0 -> x1, blocking collectives: none -> 22.2 us  [body(): drag = lax.all_gather(drag, 'block')]
    ppermute x4 -> x0, starting transfers between devices: 8.93 us -> none  [body(): drag = drag + lax.ppermute(drag, 'block', swap)]
    ppermute x1, starting transfers between devices: 3.03 us -> 8.04 us  [body(): gradient_left = lax.ppermute(gradient, 'block', up[:-1])]
    ppermute x4 -> x0, waiting for transfers between devices: 4.18 us -> none  [body(): drag = drag + lax.ppermute(drag, 'block', swap)]
    ppermute x1, waiting for transfers between devices: 7.38 us -> 4.82 us  [body(): left = lax.ppermute(tail, 'block', up)]
    add x4 -> x0, other arithmetic: 0.64 us -> none  [body(): drag = drag + lax.ppermute(drag, 'block', swap)]
  transfers between devices with their start and end apart: 8 -> 4, of which waited for: 3 -> 1; matrix products, arithmetic and copies ran while one was open for 5% -> 3% of each run, Pallas kernels for 9% -> 3%
where the time goes in v2:
time: 63.4 us; the launch traced here: 63.1 us
  blocking collectives  22.2 us (35%)
  starting transfers between devices  14.9 us (24%)
  Pallas kernels  13.6 us (21%)
  waiting for transfers between devices  4.82 us (8%)
  between operations  2.61 us (4%)
  local copies, waits for them, and re-layouts  2.55 us (4%)
  other arithmetic  2.39 us (4%)
    all_gather x1, blocking collectives, body(): drag = lax.all_gather(drag, 'block')  22.2 us
    ppermute x1, starting transfers between devices, body(): gradient_left = lax.ppermute(gradient, 'block', up[:-1])  8.04 us
    pallas_call x1, Pallas kernels, body(): pl.pallas_call(functools.partial(forward_kernel, home), out_shape=[jax.Sh...  7.29 us
    ppermute x1, starting transfers between devices, body(): right = lax.ppermute(head, 'block', down)  5.06 us
    ppermute x1, waiting for transfers between devices, body(): left = lax.ppermute(tail, 'block', up)  4.82 us
    pallas_call x1, Pallas kernels, body(): pl.pallas_call(functools.partial(backward_kernel, home), out_shape=jax.Sh...  2.86 us
    pallas_call x1, Pallas kernels, place(): pl.pallas_call(functools.partial(place_kernel, blocks, reach), out_shape=...  1.76 us
    pallas_call x1, Pallas kernels, body(): pl.pallas_call(functools.partial(scale_kernel, home, cells), out_shape=ja...  1.71 us
  transfers between devices with their start and end apart: 4, of which 1 were waited for; matrix products, arithmetic and copies ran while one was open for 3% of the time, Pallas kernels for 3%

profile of v2, /device:TPU:0, one launch (start us, length us, event | category | flops | bytes accessed | tf_op | source)
XLA Modules:
  0.0 63.1 jit_solution(9182326127850006232)
XLA Ops:
  0.6 0.0 copy-start
  0.6 0.0 copy-start.5
  0.7 0.9 %compare_select_fusion.marked = f32[12,8,128]{2,1,0:T(8,128)S(1)} fusion(f32[12,8,128]{2,1,0:T(8,128)} %param.7, s32[12,8,128]{2,1,0:T(8,128)} %param.8), kind=kLoop, calls=%fused_computation.3 | loop fusion | flops 24576 | bytes 147456 | tf_op jit(solution)/shard_map/jit(_where)/select_n | solution.py:350
  1.6 1.3 %fusion = (f32[19,7,8,128]{3,2,1,0:T(8,128)S(1)}, f32[19,7,8,128]{3,2,1,0:T(8,128)S(1)}) fusion(f32[19,12,8,128]{3,2,1,0:T(8,128)} %pops.1), kind=kLoop, calls=%fused_computation.11 | loop fusion | bytes 2179072 | tf_op jit(solution)/shard_map/slice | solution.py:352
  2.9 0.5 collective-permute-start.2
  3.5 5.1 %collective-permute-start.3 = (f32[20,7,8,128]{3,2,1,0:T(8,128)S(1)}, f32[20,7,8,128]{3,2,1,0:T(8,128)S(1)}, u32[]{:S(2)}, u32[]{:S(2)}) collective-permute-start(f32[20,7,8,128]{3,2,1,0:T(8,128)S(1)} %pad_maximum_fusion.2), channel_id=1, source_target_pairs={{1,0},{2,1},{3,2},{4,3},{5,4},{6,5},{7,6},{8,7},{9,8},{10,9},{11,1... | collective-permute-start | bytes 1720328 | tf_op jit(solution)/shard_map/ppermute | solution.py:354
  8.5 0.0 copy-done.5
  8.5 0.1 convert_reduce_fusion
  8.7 0.6 fusion.1
  10.5 0.6 %compare_reduce_fusion = pred[]{:T(512)} fusion(s32[17]{0:T(128)S(1)} %convert_reduce_fusion), kind=kLoop, calls=%fused_computation.8 | loop fusion | flops 84 | bytes 69 | tf_op jit(solution)/shard_map/reduce_or | solution.py:359
  11.1 4.8 %collective-permute-done.2.left = f32[20,7,8,128]{3,2,1,0:T(8,128)S(1)} collective-permute-done((f32[20,7,8,128]{3,2,1,0:T(8,128)S(1)}, f32[20,7,8,128]{3,2,1,0:T(8,128)S(1)}, u32[]{:S(2)}, u32[]{:S(2)}) %collective-permute-start.2) | collective-permute-done | bytes 573472 | tf_op jit(solution)/shard_map/ppermute | solution.py:353
  15.9 0.0 collective-permute-done.3.right
  15.9 0.0 copy-done
  15.9 7.3 %forward_steps.1 = (f32[19,20,8,128]{3,2,1,0:T(8,128)}, f32[16,26,8,128]{3,2,1,0:T(8,128)S(1)}, f32[26,8,128]{2,1,0:T(8,128)S(1)}, s32[26,8,128]{2,1,0:T(8,128)S(1)}, f32[8,128]{1,0:T(8,128)S(1)}) custom-call(f32[19,12,8,128]{3,2,1,0:T(8,128)S(1)} %copy-done, f32[12,8,128]{2,1,0:T(8,128)S(1)} %compare_select_fusion.marked, ...), custom_call_target="tpu_custom_call" | custom-call | flops 25000000 | bytes 6000000 | tf_op jit(solution)/shard_map/forward_steps/pallas_call | solution.py:364
  23.2 2.9 %backward_steps.1.own = f32[12,8,128]{2,1,0:T(8,128)S(1)} custom-call(f32[16,26,8,128]{3,2,1,0:T(8,128)S(1)} %get-tuple-element.24.history, f32[26,8,128]{2,1,0:T(8,128)S(1)} %get-tuple-element.25.opens, s32[26,8,128]{2,1,0:T(8,128)S(1)} %get-tuple-element.26.words, f32[12,8,128]{2,1,0:T(8,128)S(1)} %compare_select_fusion.marked), custom_call_target="tpu_custom_call" | custom-call | flops 15000000 | bytes 4000000 | tf_op jit(solution)/shard_map/backward_steps/pallas_call | solution.py:389
  26.1 0.0 copy-start.1
  26.1 1.3 %collective-permute-start.5 = (f32[12,8,128]{2,1,0:T(8,128)S(1)}, f32[12,8,128]{2,1,0:T(8,128)S(1)}, u32[]{:S(2)}, u32[]{:S(2)}) collective-permute-start(f32[12,8,128]{2,1,0:T(8,128)S(1)} %backward_steps.1.own), channel_id=1, source_target_pairs={{1,0},{2,1},{3,2},{4,3},{5,4},{6,5},{7,6},{8,7},{9,8},{10,9},{11,1... | collective-permute-start | bytes 147464 | tf_op jit(solution)/shard_map/ppermute | solution.py:405
  27.4 8.0 %collective-permute-start.4 = (f32[12,8,128]{2,1,0:T(8,128)S(1)}, f32[12,8,128]{2,1,0:T(8,128)S(1)}, u32[]{:S(2)}, u32[]{:S(2)}) collective-permute-start(f32[12,8,128]{2,1,0:T(8,128)S(1)} %backward_steps.1.own), channel_id=1, source_target_pairs={{0,1},{1,2},{2,3},{3,4},{4,5},{5,6},{6,7},{7,8},{8,9},{9,10},{10,1... | collective-permute-start | bytes 147464 | tf_op jit(solution)/shard_map/ppermute | solution.py:404
  35.4 0.6 %pad_add_fusion.where = s32[2]{0:T(128)S(1)} fusion(s32[1]{0:T(128)S(6)} %sub.8, s32[1]{0:T(128)} %get-tuple-element.31), kind=kLoop, calls=%fused_computation.9 | loop fusion | flops 2 | bytes 16 | tf_op jit(solution)/shard_map/stack | solution.py:362
  36.7 0.0 copy-done.1
  36.7 1.8 %conditional.1 = (f32[19,20,8,128]{3,2,1,0:T(8,128)S(1)}) conditional(s32[]{:T(128)} %convert_element_type.7, (s32[2]{0:T(128)S(1)}, f32[19,20,8,128]{3,2,1,0:T(8,128)}) %tuple.14, (f32[19,20,8,128]{3,2,1,0:T(8,128)}, s32[2]{0:T(128)S(1)}) %tuple.15), branch_computations={%region_2.3_spmd, %region_3.4_spmd} | conditional | flops 1400832 | bytes 18142296 | solution.py:425
  36.8 1.8 %place_populations.2 = f32[19,20,8,128]{3,2,1,0:T(8,128)S(1)} custom-call(s32[2]{0:T(128)S(1)} %get-tuple-element.8.where, f32[19,20,8,128]{3,2,1,0:T(8,128)} %get-tuple-element.12.source), custom_call_target="tpu_custom_call" | custom-call | bytes 3200000 | tf_op jit(solution)/shard_map/cond/branch_0_fun/place_populations/pallas_call | solution.py:310
  38.5 0.0 copy-start.2
  38.5 22.2 %all-gather = f32[128,128]{1,0:T(8,128)} all-gather(f32[8,128]{1,0:T(8,128)S(1)} %get-tuple-element.23), channel_id=2, replica_groups=mesh['group'=2,'block'=16] {'block'}, dimensions={0}, use_global_device_ids=true | all-gather | bytes 69632 | tf_op jit(solution)/shard_map/all_gather | solution.py:387
  60.8 0.0 collective-permute-done.5.right
  60.8 0.0 copy-start.3
  60.8 0.0 collective-permute-done.4.left
  60.8 0.0 copy-start.4
  60.8 0.6 copy-done.3
  61.4 0.0 copy-done.4
  61.4 1.7 %place_gradient.1 = f32[20,8,128]{2,1,0:T(8,128)} custom-call(s32[2]{0:T(128)S(1)} %pad_add_fusion.where, f32[16,8,128]{2,1,0:T(8,128)} %bitcast.5, f32[12,8,128]{2,1,0:T(8,128)} %copy-done.4, f32[12,8,128]{2,1,0:T(8,128)} %copy-done.1, f32[12,8,128]{2,1,0:T(8,128)} %copy-done.3), custom_call_target="tpu_custom_call" | custom-call | tf_op jit(solution)/shard_map/place_gradient/pallas_call | solution.py:407
  63.1 0.0 copy-done.2
  (4 shorter events, 0.1 us)
Async XLA Ops:
  0.6 15.3 %copy-start = (f32[19,12,8,128]{3,2,1,0:T(8,128)S(1)}, f32[19,12,8,128]{3,2,1,0:T(8,128)}, u32[]{:S(2)}) copy-start(f32[19,12,8,128]{3,2,1,0:T(8,128)} %pops.1) | copy-start | bytes 2801668
  0.6 7.9 %copy-start.5 = (s32[48]{0:T(128)S(1)}, s32[48]{0:T(128)}, u32[]{:S(2)}) copy-start(s32[48]{0:T(128)} %param.9) | copy-start | bytes 580
  2.9 13.0 %collective-permute-start.2 = (f32[20,7,8,128]{3,2,1,0:T(8,128)S(1)}, f32[20,7,8,128]{3,2,1,0:T(8,128)S(1)}, u32[]{:S(2)}, u32[]{:S(2)}) collective-permute-start(f32[20,7,8,128]{3,2,1,0:T(8,128)S(1)} %pad_maximum_fusion.1), channel_id=1, source_target_pairs={{0,1},{1,2},{2,3},{3,4},{4,5},{5,6},{6,7},{7,8},{8,9},{9,10},{10,1... | collective-permute-start | bytes 1720328 | tf_op jit(solution)/shard_map/ppermute | solution.py:353
  3.5 12.5 %collective-permute-start.3 = (f32[20,7,8,128]{3,2,1,0:T(8,128)S(1)}, f32[20,7,8,128]{3,2,1,0:T(8,128)S(1)}, u32[]{:S(2)}, u32[]{:S(2)}) collective-permute-start(f32[20,7,8,128]{3,2,1,0:T(8,128)S(1)} %pad_maximum_fusion.2), channel_id=1, source_target_pairs={{1,0},{2,1},{3,2},{4,3},{5,4},{6,5},{7,6},{8,7},{9,8},{10,9},{11,1... | collective-permute-start | bytes 1720328 | tf_op jit(solution)/shard_map/ppermute | solution.py:354
  26.1 10.6 %copy-start.1 = (f32[12,8,128]{2,1,0:T(8,128)}, f32[12,8,128]{2,1,0:T(8,128)S(1)}, u32[]{:S(2)}) copy-start(f32[12,8,128]{2,1,0:T(8,128)S(1)} %backward_steps.1.own) | copy-start | bytes 147460
  26.1 34.7 %collective-permute-start.5 = (f32[12,8,128]{2,1,0:T(8,128)S(1)}, f32[12,8,128]{2,1,0:T(8,128)S(1)}, u32[]{:S(2)}, u32[]{:S(2)}) collective-permute-start(f32[12,8,128]{2,1,0:T(8,128)S(1)} %backward_steps.1.own), channel_id=1, source_target_pairs={{1,0},{2,1},{3,2},{4,3},{5,4},{6,5},{7,6},{8,7},{9,8},{10,9},{11,1... | collective-permute-start | bytes 147464 | tf_op jit(solution)/shard_map/ppermute | solution.py:405
  27.4 33.4 %collective-permute-start.4 = (f32[12,8,128]{2,1,0:T(8,128)S(1)}, f32[12,8,128]{2,1,0:T(8,128)S(1)}, u32[]{:S(2)}, u32[]{:S(2)}) collective-permute-start(f32[12,8,128]{2,1,0:T(8,128)S(1)} %backward_steps.1.own), channel_id=1, source_target_pairs={{0,1},{1,2},{2,3},{3,4},{4,5},{5,6},{6,7},{7,8},{8,9},{9,10},{10,1... | collective-permute-start | bytes 147464 | tf_op jit(solution)/shard_map/ppermute | solution.py:404
  38.5 24.6 %copy-start.2 = (f32[19,20,8,128]{3,2,1,0:T(8,128)}, f32[19,20,8,128]{3,2,1,0:T(8,128)S(1)}, u32[]{:S(2)}) copy-start(f32[19,20,8,128]{3,2,1,0:T(8,128)S(1)} %get-tuple-element.33) | copy-start | bytes 4669444
  60.8 0.6 copy-start.3
  60.8 0.6 %copy-start.4 = (f32[12,8,128]{2,1,0:T(8,128)}, f32[12,8,128]{2,1,0:T(8,128)S(1)}, u32[]{:S(2)}) copy-start(f32[12,8,128]{2,1,0:T(8,128)S(1)} %collective-permute-done.4.left) | copy-start | bytes 147460
